TPU v7x, 32 devices: a whole 2x2x4 slice. The times are simulated.
32 devices in a mesh: dp: 4 (over z), expert: 4 (over x, core), tensor: 2 (over y).
Axes of the slice: x: 2, y: 2, z: 4, core: 2. Of those that a mesh axis runs over, the one named last changes fastest.
Arguments:
- tokens: bfloat16 [128, 4096], P(('dp', 'expert')), may hold values from -6 to 6
- grad_out: bfloat16 [128, 4096], P(('dp', 'expert')), may hold values from -6 to 6
- slot_token: int32 [16, 32], P(('dp', 'expert')), may hold values from 0 to 31, as said below
- slot_count: int32 [16], P(('dp', 'expert')), may hold values from 16 to 32, as said below
- slot_gate: float32 [16, 32], P(('dp', 'expert')), may hold values from 0.05 to 1
- w_gate: bfloat16 [4, 4096, 768], P('expert', 'dp', 'tensor'), may hold values from -0.09375 to 0.09375
- w_up: bfloat16 [4, 4096, 768], P('expert', 'dp', 'tensor'), may hold values from -0.09375 to 0.09375
- w_down: bfloat16 [4, 768, 4096], P('expert', 'tensor', 'dp'), may hold values from -0.21875 to 0.21875
Outputs:
- grad_tokens: bfloat16 [128, 4096], P(('dp', 'expert'))
- grad_gate: float32 [16, 32], P(('dp', 'expert'))
- grad_w_gate: bfloat16 [4, 4096, 768], P('expert', 'dp', 'tensor')
- grad_w_up: bfloat16 [4, 4096, 768], P('expert', 'dp', 'tensor')
- grad_w_down: bfloat16 [4, 768, 4096], P('expert', 'tensor', 'dp')
Inputs may be any that keep to these rules, and one draw needn't show every extreme that they name: `slot_token`: the 32 entries of one list are distinct, and a token lies in at most 4 lists of its index of dp. Slots from slot_count[r] on are unused.
All inputs are finite; a program needn't handle non-finite values.
Results may differ from a plain program's by a relative error of at most 0.015.
Values may be sent and summed in bfloat16 or wider, within the bound.
A program may use at most 64 MiB of HBM per device.

v0:
```python
import jax
import jax.numpy as jnp
from jax import lax
from jax.sharding import PartitionSpec as P


def swish_slope(pre_act):
    sigmoid_value = jax.nn.sigmoid(pre_act)
    return sigmoid_value * (1.0 + pre_act * (1.0 - sigmoid_value))


def block_total(block_parts):
    rounded = lax.optimization_barrier(block_parts.astype(jnp.bfloat16))
    return jnp.sum(rounded.astype(jnp.float32), axis=0)


def shards(tokens, grad_out, slot_token, slot_count, slot_gate, w_gate, w_up, w_down):
    gathered_x, gathered_dy = (
        lax.all_gather(tokens, "expert", axis=0, tiled=True),
        lax.all_gather(grad_out, "expert", axis=0, tiled=True),
    )
    capacity = slot_token.shape[1]
    slot_index = slot_token[0]
    is_live = jnp.arange(capacity) < slot_count[0]
    gate_live = jnp.where(is_live, slot_gate[0], 0.0)
    rows_x = jnp.take(gathered_x, slot_index, axis=0)
    rows_dy = jnp.take(gathered_dy, slot_index, axis=0)
    cols_x, cols_dy = (
        lax.all_to_all(rows_x, "dp", split_axis=1, concat_axis=0, tiled=True),
        lax.all_to_all(rows_dy, "dp", split_axis=1, concat_axis=0, tiled=True),
    )
    block_width = w_gate.shape[1]
    hidden_width = w_gate.shape[2]
    dp_count = lax.axis_size("dp")
    by_last = (((1,), (1,)), ((), ()))
    by_first = (((0,), (0,)), ((), ()))
    full_gate, full_up, full_down = (
        lax.all_gather(w_gate, "dp", axis=1, tiled=True),
        lax.all_gather(w_up, "dp", axis=1, tiled=True),
        lax.all_gather(w_down, "dp", axis=2, tiled=True),
    )
    blocks_x = rows_x.reshape(capacity, dp_count, block_width)
    blocks_dy = rows_dy.reshape(capacity, dp_count, block_width)
    pre_gate = block_total(
        jnp.einsum(
            "cnd,ndf->ncf",
            blocks_x,
            full_gate[0].reshape(dp_count, block_width, hidden_width),
            preferred_element_type=jnp.float32,
        )
    )
    pre_up = block_total(
        jnp.einsum(
            "cnd,ndf->ncf",
            blocks_x,
            full_up[0].reshape(dp_count, block_width, hidden_width),
            preferred_element_type=jnp.float32,
        )
    )
    back_grad = block_total(
        jnp.einsum(
            "cnd,fnd->ncf",
            blocks_dy,
            full_down[0].reshape(hidden_width, dp_count, block_width),
            preferred_element_type=jnp.float32,
        )
    )
    hidden = jax.nn.silu(pre_gate) * pre_up
    gate_part_sum = jnp.sum(hidden * back_grad, axis=1)
    d_hidden = gate_live[:, None] * back_grad
    d_up = (d_hidden * jax.nn.silu(pre_gate)).astype(jnp.bfloat16)
    d_gate = (d_hidden * pre_up * swish_slope(pre_gate)).astype(jnp.bfloat16)
    scaled = (gate_live[:, None] * hidden).astype(jnp.bfloat16)
    all_gate, all_up, all_scaled = (
        lax.all_gather(d_gate, "dp", axis=0, tiled=True),
        lax.all_gather(d_up, "dp", axis=0, tiled=True),
        lax.all_gather(scaled, "dp", axis=0, tiled=True),
    )
    gate_total = lax.psum(gate_part_sum, "tensor")
    grad_gate = jnp.where(is_live, gate_total, 0.0)[None, :]
    grad_w_gate = lax.dot_general(
        cols_x, all_gate, by_first, preferred_element_type=jnp.float32
    ).astype(jnp.bfloat16)[None]
    grad_w_up = lax.dot_general(
        cols_x, all_up, by_first, preferred_element_type=jnp.float32
    ).astype(jnp.bfloat16)[None]
    grad_w_down = lax.dot_general(
        all_scaled, cols_dy, by_first, preferred_element_type=jnp.float32
    ).astype(jnp.bfloat16)[None]
    partial_rows = lax.dot_general(
        d_gate, full_gate[0], by_last, preferred_element_type=jnp.float32
    ) + lax.dot_general(d_up, full_up[0], by_last, preferred_element_type=jnp.float32)
    d_rows = lax.psum(partial_rows.astype(jnp.bfloat16), "tensor")
    scattered = (
        jnp.zeros((gathered_x.shape[0], d_rows.shape[1]), jnp.float32)
        .at[slot_index]
        .set(d_rows.astype(jnp.float32))
    )
    returned = lax.psum_scatter(
        scattered.astype(jnp.bfloat16), "expert", scatter_dimension=0, tiled=True
    )
    return (returned, grad_gate, grad_w_gate, grad_w_up, grad_w_down)


def solution(mesh):
    return jax.shard_map(
        shards,
        mesh=mesh,
        in_specs=(
            P(("dp", "expert"), None),
            P(("dp", "expert"), None),
            P(("dp", "expert"), None),
            P(("dp", "expert")),
            P(("dp", "expert"), None),
            P("expert", "dp", "tensor"),
            P("expert", "dp", "tensor"),
            P("expert", "tensor", "dp"),
        ),
        out_specs=(
            P(("dp", "expert"), None),
            P(("dp", "expert"), None),
            P("expert", "dp", "tensor"),
            P("expert", "dp", "tensor"),
            P("expert", "tensor", "dp"),
        ),
        check_vma=False,
    )
```

profile of v0, /device:TPU:0, one launch (start us, length us, event | category | flops | bytes accessed | tf_op | source)
XLA Modules:
  0.0 281.4 jit_solution(10477473366958730562)
XLA Ops:
  7.2 0.0 copy-start.3
  7.2 0.0 copy-start.7
  7.2 0.0 copy-start.4
  7.2 0.0 all-gather.4.cloned.1.call-start
  7.2 2.3 copy.23
  9.5 0.0 all-gather.4.cloned.1.call-update
  9.6 0.0 all-gather.8.cloned.1.call-start
  9.6 0.7 all-gather.8.cloned.1.call-update
  10.3 0.0 all-gather.6.cloned.1.call-start
  10.4 0.7 all-gather.6.cloned.1.call-update
  11.0 0.0 copy-done.3
  11.1 7.2 %all_gather.24 = bf16[32,4096]{1,0:T(8,128)(2,1)S(1)} all-gather(bf16[8,4096]{1,0:T(8,128)(2,1)S(1)} %copy-done.3), channel_id=1, replica_groups=mesh['dp'=4,'expert'=4,'tensor'=2] {'expert'}, dimensions={0}, use_global_device_ids=true | all-gather | bytes 327680 | tf_op jit(solution)/shard_map/all_gather | solution.py:20
  18.2 0.0 copy-done.7
  18.3 0.7 gather_fusion
  19.0 0.0 copy-done.4
  19.0 0.0 copy-start.6
  19.0 5.9 %all_gather.26 = bf16[32,4096]{1,0:T(8,128)(2,1)S(1)} all-gather(bf16[8,4096]{1,0:T(8,128)(2,1)S(1)} %copy-done.4), channel_id=1, replica_groups=mesh['dp'=4,'expert'=4,'tensor'=2] {'expert'}, dimensions={0}, use_global_device_ids=true | all-gather | bytes 327680 | tf_op jit(solution)/shard_map/all_gather | solution.py:19
  24.9 0.7 gather_fusion.1
  25.6 0.1 broadcast_select_fusion.1
  25.7 0.7 copy.38
  26.4 4.9 %all-to-all-start = ((bf16[32,4,1024]{2,0,1:T(8,128)(2,1)}), bf16[32,4,1024]{2,0,1:T(8,128)(2,1)}, u32[]{:S(2)}, u32[]{:S(2)}) async-start(bf16[32,4,1024]{2,0,1:T(8,128)(2,1)} %bitcast.54), calls=%async_computation.1 | async-start | bytes 524288 | tf_op jit(solution)/shard_map/all_to_all | solution.py:29
  31.3 0.0 all-reduce.2.cloned.1.call-start
  32.0 0.7 copy.39
  32.7 0.0 copy-done.6
  32.7 0.5 compare_select_fusion.3
  33.2 48.7 %all-gather.4.cloned.1.call-done = bf16[1,384,4096]{1,2,0:T(8,128)(2,1)} async-done(((bf16[1,384,1024]{1,2,0:T(8,128)(2,1)}), bf16[1,384,4096]{1,2,0:T(8,128)(2,1)}) %all-gather.4.cloned.1.call-update) | async-done | bytes 3145744 | tf_op jit(solution)/shard_map/all_gather | solution.py:40
  81.9 2.4 convolution_convert_fusion.5
  84.3 61.3 %all-gather.8.cloned.1.call-done = bf16[1,4096,384]{2,1,0:T(8,128)(2,1)} async-done(((bf16[1,1024,384]{2,1,0:T(8,128)(2,1)}), bf16[1,4096,384]{2,1,0:T(8,128)(2,1)}) %all-gather.8.cloned.1.call-update) | async-done | bytes 3145744 | tf_op jit(solution)/shard_map/all_gather | solution.py:38
  145.6 0.0 copy-start
  145.6 3.2 %convolution_convert_fusion.3 = bf16[4,32,384]{2,1,0:T(8,128)(2,1)} fusion(bf16[4,1024,384]{2,1,0:T(8,128)(2,1)} %bitcast.58, bf16[4,4,8,1024]{3,2,1,0:T(8,128)(2,1)S(1)} %bitcast.61), kind=kOutput, calls=%fused_computation.14 | convolution fusion | flops 100712448 | bytes 3506176 | tf_op jit(solution)/shard_map/cnd,ndf->ncf/dot_general | solution.py:45
  148.9 0.0 copy-start.2
  148.9 60.5 %all-gather.6.cloned.1.call-done = bf16[1,4096,384]{2,1,0:T(8,128)(2,1)} async-done(((bf16[1,1024,384]{2,1,0:T(8,128)(2,1)}), bf16[1,4096,384]{2,1,0:T(8,128)(2,1)}) %all-gather.6.cloned.1.call-update) | async-done | bytes 3145744 | tf_op jit(solution)/shard_map/all_gather | solution.py:39
  209.4 0.0 copy-start.5
  209.4 0.0 copy-start.1
  209.4 2.6 convolution_convert_fusion.4
  211.9 0.0 copy-done.2
  212.0 0.0 copy-done.5
  212.0 0.1 multiply_reduce_fusion
  212.1 0.0 copy-done
  212.1 1.1 fusion.2
  213.2 0.0 copy-start.8
  213.2 0.0 copy-done.1
  213.2 1.8 fusion
  215.0 0.0 all-reduce.2.cloned.1.call-update
  215.0 0.0 all-to-all-done
  215.0 3.4 %all-to-all-start.1 = ((bf16[32,4,1024]{2,0,1:T(8,128)(2,1)}), bf16[32,4,1024]{2,0,1:T(8,128)(2,1)S(1)}, u32[]{:S(2)}, u32[]{:S(2)}) async-start(bf16[32,4,1024]{2,0,1:T(8,128)(2,1)} %bitcast.55), calls=%async_computation.2 | async-start | bytes 524288 | tf_op jit(solution)/shard_map/all_to_all | solution.py:30
  218.5 0.0 reduce-scatter.2.cloned.1.call-start
  218.5 0.0 copy-done.8
  218.5 16.1 %all_gather.29 = bf16[128,384]{1,0:T(8,128)(2,1)S(1)} all-gather(bf16[32,384]{1,0:T(8,128)(2,1)S(1)} %get-tuple-element.7), channel_id=1, replica_groups=mesh['dp'=4,'expert'=4,'tensor'=2] {'dp'}, dimensions={0}, use_global_device_ids=true | all-gather | bytes 122880 | tf_op jit(solution)/shard_map/all_gather | solution.py:75
  234.6 2.2 fusion.4
  236.8 0.2 all-reduce.2.cloned.1.call-done
  237.0 1.5 scatter_custom_fusion
  238.5 0.7 convert_element_type.55
  239.2 0.0 reduce-scatter.2.cloned.1.call-update
  239.3 13.4 %all_gather.30 = bf16[128,384]{1,0:T(8,128)(2,1)S(1)} all-gather(bf16[32,384]{1,0:T(8,128)(2,1)S(1)} %get-tuple-element.9), channel_id=1, replica_groups=mesh['dp'=4,'expert'=4,'tensor'=2] {'dp'}, dimensions={0}, use_global_device_ids=true | all-gather | bytes 122880 | tf_op jit(solution)/shard_map/all_gather | solution.py:76
  252.6 4.9 %psum.15 = f32[32]{0:T(128)S(1)} all-reduce(f32[32]{0:T(128)S(1)} %get-tuple-element.6), channel_id=1, replica_groups=mesh['dp'=4,'expert'=4,'tensor'=2] {'tensor'}, use_global_device_ids=true, to_apply=%region_7.9 | all-reduce | flops 32 | bytes 256 | tf_op jit(solution)/shard_map/psum | solution.py:79
  257.6 13.3 %all_gather.31 = bf16[128,384]{1,0:T(8,128)(2,1)S(1)} all-gather(bf16[32,384]{1,0:T(8,128)(2,1)S(1)} %get-tuple-element.8), channel_id=1, replica_groups=mesh['dp'=4,'expert'=4,'tensor'=2] {'dp'}, dimensions={0}, use_global_device_ids=true | all-gather | bytes 122880 | tf_op jit(solution)/shard_map/all_gather | solution.py:77
  270.9 2.2 fusion.5
  273.1 0.0 all-to-all-done.1
  273.1 1.3 fusion.6
  274.4 0.5 fusion.11
  274.9 0.0 reduce-scatter.2.cloned.1.call-done
  (6 shorter events, 0.1 us)
Async XLA Ops:
  7.2 3.9 %copy-start.3 = (bf16[8,4096]{1,0:T(8,128)(2,1)S(1)}, bf16[8,4096]{1,0:T(8,128)(2,1)}, u32[]{:S(2)}) copy-start(bf16[8,4096]{1,0:T(8,128)(2,1)} %param.11) | copy-start | bytes 196612
  7.2 11.1 %copy-start.7 = (s32[1,32]{1,0:T(1,128)S(1)}, s32[1,32]{1,0:T(1,128)}, u32[]{:S(2)}) copy-start(s32[1,32]{1,0:T(1,128)} %param.12) | copy-start | bytes 388
  7.2 11.8 %copy-start.4 = (bf16[8,4096]{1,0:T(8,128)(2,1)S(1)}, bf16[8,4096]{1,0:T(8,128)(2,1)}, u32[]{:S(2)}) copy-start(bf16[8,4096]{1,0:T(8,128)(2,1)} %param.10) | copy-start | bytes 196612
  7.2 74.7 %all-gather.4.cloned.1.call-start = ((), (), s32[]{:S(2)}) async-start(), calls=%async_computation.3 | async-start | bytes 3932160 | tf_op jit(solution)/shard_map/all_gather | solution.py:40
  9.6 136.1 %all-gather.8.cloned.1.call-start = ((), (), s32[]{:S(2)}) async-start(), calls=%async_computation.5 | async-start | bytes 3932160 | tf_op jit(solution)/shard_map/all_gather | solution.py:38
  10.3 199.1 %all-gather.6.cloned.1.call-start = ((), (), s32[]{:S(2)}) async-start(), calls=%async_computation.4 | async-start | bytes 3932160 | tf_op jit(solution)/shard_map/all_gather | solution.py:39
  19.0 13.7 %copy-start.6 = (f32[1,32]{1,0:T(1,128)S(1)}, f32[1,32]{1,0:T(1,128)}, u32[]{:S(2)}) copy-start(f32[1,32]{1,0:T(1,128)} %param.14) | copy-start | bytes 388
  26.4 188.6 %all-to-all-start = ((bf16[32,4,1024]{2,0,1:T(8,128)(2,1)}), bf16[32,4,1024]{2,0,1:T(8,128)(2,1)}, u32[]{:S(2)}, u32[]{:S(2)}) async-start(bf16[32,4,1024]{2,0,1:T(8,128)(2,1)} %bitcast.54), calls=%async_computation.1 | async-start | bytes 524288 | tf_op jit(solution)/shard_map/all_to_all | solution.py:29
  31.3 205.7 %all-reduce.2.cloned.1.call-start = ((), (), s32[]{:S(2)}) async-start(), calls=%async_computation.6 | async-start | bytes 524288 | tf_op jit(solution)/shard_map/psum | solution.py:93
  145.6 66.5 %copy-start = (bf16[1,4096,384]{2,1,0:T(8,128)(2,1)S(1)}, bf16[1,4096,384]{2,1,0:T(8,128)(2,1)}, u32[]{:S(2)}) copy-start(bf16[1,4096,384]{2,1,0:T(8,128)(2,1)} %all-gather.8.cloned.1.call-done) | copy-start | bytes 9437188
  148.9 63.1 %copy-start.2 = (bf16[4,32,384]{2,1,0:T(8,128)(2,1)S(1)}, bf16[4,32,384]{2,1,0:T(8,128)(2,1)}, u32[]{:S(2)}) copy-start(bf16[4,32,384]{2,1,0:T(8,128)(2,1)} %convolution_convert_fusion.3) | copy-start | bytes 294916
  209.4 2.6 copy-start.5
  209.4 3.8 %copy-start.1 = (bf16[1,4096,384]{2,1,0:T(8,128)(2,1)S(1)}, bf16[1,4096,384]{2,1,0:T(8,128)(2,1)}, u32[]{:S(2)}) copy-start(bf16[1,4096,384]{2,1,0:T(8,128)(2,1)} %all-gather.6.cloned.1.call-done) | copy-start | bytes 9437188
  213.2 5.3 %copy-start.8 = (s32[1,32]{1,0:T(1,128)S(1)}, s32[1,32]{1,0:T(1,128)}, u32[]{:S(2)}) copy-start(s32[1,32]{1,0:T(1,128)} %param.12) | copy-start | bytes 388
  215.0 58.1 %all-to-all-start.1 = ((bf16[32,4,1024]{2,0,1:T(8,128)(2,1)}), bf16[32,4,1024]{2,0,1:T(8,128)(2,1)S(1)}, u32[]{:S(2)}, u32[]{:S(2)}) async-start(bf16[32,4,1024]{2,0,1:T(8,128)(2,1)} %bitcast.55), calls=%async_computation.2 | async-start | bytes 524288 | tf_op jit(solution)/shard_map/all_to_all | solution.py:30
  218.5 56.4 %reduce-scatter.2.cloned.1.call-start = ((), (), s32[]{:S(2)}) async-start(), calls=%async_computation.7 | async-start | bytes 327680 | tf_op jit(solution)/shard_map/reduce_scatter | solution.py:99
Sparse Core Ops, SparseCore 0:
  10.2 71.6 all-gather.3
  83.5 62.1 all-gather.7
  147.2 62.1 all-gather.5
  215.2 21.8 all-reduce.1
  240.1 20.0 reduce-scatter.1
where the time goes:
time: 282 us; the launch traced here: 281 us
  waiting for transfers between devices  172 us (61%)
  blocking collectives  60.7 us (22%)
  matrix products  16.8 us (6%)
  between operations  14.6 us (5%)
  starting transfers between devices  8.49 us (3%)
  local copies, waits for them, and re-layouts  5.2 us (2%)
  other arithmetic  3.54 us (1%)
    all_gather x1, waiting for transfers between devices, shards(): lax.all_gather(w_gate, 'dp', axis=1, tiled=True)  61.3 us
    all_gather x1, waiting for transfers between devices, shards(): lax.all_gather(w_up, 'dp', axis=1, tiled=True)  60.5 us
    all_gather x1, waiting for transfers between devices, shards(): lax.all_gather(w_down, 'dp', axis=2, tiled=True)  48.7 us
    all_gather x1, blocking collectives, shards(): lax.all_gather(d_gate, 'dp', axis=0, tiled=True)  16.1 us
    all_gather x1, blocking collectives, shards(): lax.all_gather(d_up, 'dp', axis=0, tiled=True)  13.4 us
    all_gather x1, blocking collectives, shards(): lax.all_gather(scaled, 'dp', axis=0, tiled=True)  13.3 us
    all_gather x1, blocking collectives, shards(): lax.all_gather(grad_out, 'expert', axis=0, tiled=True)  7.19 us
    all_gather x1, blocking collectives, shards(): lax.all_gather(tokens, 'expert', axis=0, tiled=True)  5.86 us
  transfers between devices with their start and end apart: 7, of which 4 were waited for; matrix products, arithmetic and copies ran while one was open for 8% of the time, Pallas kernels for 0%

commit v1 on v0

v1 whole, which is shorter than its diff:
```python
import functools

import jax
import jax.numpy as jnp
from jax import lax
from jax.experimental import pallas as pl
from jax.experimental.pallas import tpu as pltpu
from jax.sharding import PartitionSpec as P

MESH = pl.DeviceIdType.MESH
F32 = jnp.float32
BF16 = jnp.bfloat16


def nn(a, b):
    return lax.dot_general(a, b, (((1,), (0,)), ((), ())), preferred_element_type=F32)


def nt(a, b):
    return lax.dot_general(a, b, (((1,), (1,)), ((), ())), preferred_element_type=F32)


def kernel(
    n, ex, tn,
    x_ref, dy_ref, slot_ref, count_ref, gate_ref, wg_hbm, wu_hbm, wd_hbm,
    gt_ref, gg_ref, gwg_hbm, gwu_hbm, gwd_hbm,
    wg, wu, wd, owg, owu, owd, src, full, xs, ys, xt, ps, pr, dgu, dsc,
    dsend, drecv, esend, erecv, gsend, grecv,
    w_sem, o_sem, a1s, a1r, a2s, a2r, bs, br, cs, cr, ss, sr, ds_, dr, es, er, gs, gr,
):
    d = lax.axis_index("dp")
    e = lax.axis_index("expert")
    t = lax.axis_index("tensor")
    tl = x_ref.shape[0]
    bw = xs.shape[1]
    hid = wg.shape[1]
    rows = ex * tl
    half = n // tn
    cap = slot_ref.shape[1]
    chunks = a2s.shape[0]
    per = n // chunks

    def remote(s, r, ssem, rsem, dd, ee, tt):
        return pltpu.make_async_remote_copy(
            src_ref=s, dst_ref=r, send_sem=ssem, recv_sem=rsem,
            device_id=(dd, ee, tt), device_id_type=MESH,
        )

    barrier = pltpu.get_barrier_semaphore()
    greeted = 0
    for dd in range(n):
        for ee in range(ex):
            for tt in range(tn):
                if (dd and ee) or not (dd or ee or tt):
                    continue
                pl.semaphore_signal(
                    barrier, inc=1,
                    device_id=(lax.rem(d + dd, n), lax.rem(e + ee, ex), lax.rem(t + tt, tn)),
                    device_id_type=MESH,
                )
                greeted += 1

    loads = [
        pltpu.make_async_copy(wg_hbm.at[0], wg, w_sem.at[0]),
        pltpu.make_async_copy(wu_hbm.at[0], wu, w_sem.at[1]),
        pltpu.make_async_copy(wd_hbm.at[0], wd, w_sem.at[2]),
    ]
    for load in loads:
        load.start()

    for b in range(n):
        cols = slice(b * bw, (b + 1) * bw)
        both = jnp.concatenate([x_ref[:, cols].astype(F32), dy_ref[:, cols].astype(F32)], axis=0)
        src[b] = both.astype(BF16)
    full[d, e] = src[d]
    gsend[...] = jnp.zeros_like(gsend)

    pl.semaphore_wait(barrier, greeted)

    to_dp = []
    for k in range(1, n):
        p = lax.rem(d + k, n)
        c = remote(src.at[p], full.at[d, e], a1s.at[p], a1r.at[d], p, e, t)
        c.start()
        to_dp.append(c)
    to_expert = []
    for k in range(chunks):
        chunk = lax.rem(d // per + k, chunks)
        for q in range(per):
            g = chunk * per + q
            if per == 1:
                if k:
                    remote(src.at[g], full.at[g, e], a1s.at[g], a1r.at[g], g, e, t).wait_recv()
            else:
                @pl.when(g != d)
                def _():
                    remote(src.at[g], full.at[g, e], a1s.at[g], a1r.at[g], g, e, t).wait_recv()
        span = pl.ds(chunk * per, per)
        for j in range(1, ex):
            p = lax.rem(e + j, ex)
            c = remote(full.at[span, e], full.at[span, e], a2s.at[chunk, p], a2r.at[chunk, e], d, p, t)
            c.start()
            to_expert.append(c)
    for k in range(chunks):
        chunk = lax.rem(d // per + k, chunks)
        span = pl.ds(chunk * per, per)
        for j in range(1, ex):
            p = lax.rem(e + j, ex)
            remote(full.at[span, p], full.at[span, p], a2s.at[chunk, p], a2r.at[chunk, p], d, p, t).wait_recv()
    for c in to_dp:
        c.wait_send()
    for c in to_expert:
        c.wait_send()
    for g in range(n):
        wide = full[g].astype(F32)
        xs[g * rows:(g + 1) * rows, :] = wide[:, :tl].reshape(rows, bw).astype(BF16)
        ys[g * rows:(g + 1) * rows, :] = wide[:, tl:].reshape(rows, bw).astype(BF16)

    to_owner = []
    for i, (act, w, mul) in enumerate(((xs, wg, nn), (xs, wu, nn), (ys, wd, nt))):
        loads[i].wait()
        ps[i] = mul(act[...], w[...]).astype(BF16).reshape(n, rows, hid)
        for k in range(1, n):
            p = lax.rem(d + k, n)
            c = remote(ps.at[i, p], pr.at[i, d], bs.at[i, p], br.at[i, d], p, e, t)
            c.start()
            to_owner.append(c)
    xt[...] = xs[...].T

    iota_slot = lax.broadcasted_iota(jnp.int32, (1, cap), 1)
    live = iota_slot < count_ref[0]
    gate_live = jnp.where(live, gate_ref[...], 0.0)
    holds = lax.broadcasted_iota(jnp.int32, (rows, cap), 0) == slot_ref[...]
    gate_tok = jnp.sum(jnp.where(holds, gate_live, 0.0), axis=1, keepdims=True)

    sums = []
    for i in range(3):
        total = ps[i, d].astype(F32)
        for k in range(1, n):
            p = lax.rem(d + k, n)
            remote(ps.at[i, p], pr.at[i, p], bs.at[i, p], br.at[i, p], p, e, t).wait_recv()
            total = total + pr[i, p].astype(F32)
        sums.append(total)
    pre_gate, pre_up, back = sums
    sig = 1.0 / (1.0 + jnp.exp(-pre_gate))
    silu = pre_gate * sig
    hidden = silu * pre_up
    d_hidden = gate_tok * back
    dgu[d, 0] = (d_hidden * pre_up * (sig * (1.0 + pre_gate * (1.0 - sig)))).astype(BF16)
    dgu[d, 1] = (d_hidden * silu).astype(BF16)
    to_all = []
    for k in range(1, n):
        p = lax.rem(d + k, n)
        c = remote(dgu.at[d], dgu.at[d], cs.at[p], cr.at[d], p, e, t)
        c.start()
        to_all.append(c)
    dsc[d] = (gate_tok * hidden).astype(BF16)
    for k in range(1, n):
        p = lax.rem(d + k, n)
        c = remote(dsc.at[d], dsc.at[d], ss.at[p], sr.at[d], p, e, t)
        c.start()
        to_all.append(c)
    terms = jnp.sum(hidden * back, axis=1, keepdims=True)
    gsend[0:1, 0:cap] = jnp.where(
        live, jnp.sum(jnp.where(holds, terms, 0.0), axis=0, keepdims=True), 0.0
    )
    for k in range(1, tn):
        p = lax.rem(t + k, tn)
        c = remote(gsend, grecv.at[t], gs.at[p], gr.at[t], d, e, p)
        c.start()
        to_all.append(c)

    for k in range(1, n):
        p = lax.rem(d + k, n)
        remote(dgu.at[p], dgu.at[p], cs.at[p], cr.at[p], p, e, t).wait_recv()
    all_gate = dgu[:, 0].reshape(n * rows, hid)
    all_up = dgu[:, 1].reshape(n * rows, hid)
    d_rows = (nt(all_gate, wg[...]) + nt(all_up, wu[...])).reshape(n, ex, tl, bw)
    for ee in range(ex):
        for tt in range(tn):
            part = d_rows[tt * half:(tt + 1) * half, ee].reshape(half * tl, bw)
            dsend[ee * tn + tt] = part.astype(BF16)
    me = e * tn + t
    for ee in range(ex):
        for tt in range(tn):
            if ee or tt:
                pe, pt = lax.rem(e + ee, ex), lax.rem(t + tt, tn)
                c = remote(dsend.at[pe * tn + pt], drecv.at[me], ds_.at[pe * tn + pt], dr.at[me], d, pe, pt)
                c.start()
                to_all.append(c)

    owg[...] = nn(xt[...], all_gate).astype(BF16)
    stores = [pltpu.make_async_copy(owg, gwg_hbm.at[0], o_sem.at[0])]
    stores[0].start()

    total = dsend[me].astype(F32)
    for ee in range(ex):
        for tt in range(tn):
            if ee or tt:
                other = lax.rem(e + ee, ex) * tn + lax.rem(t + tt, tn)
                remote(dsend.at[other], drecv.at[other], ds_.at[other], dr.at[other], d, e, t).wait_recv()
                total = total + drecv[other].astype(F32)
    mine = d // half == t
    for q in range(half):
        part = total[q * tl:(q + 1) * tl]
        esend[q] = jnp.concatenate([part[:, :bw // 2], part[:, bw // 2:]], axis=0).astype(BF16)
        g = t * half + q
        for tt in range(tn):
            here = jnp.logical_and(g == d, t == tt)

            @pl.when(jnp.logical_not(here))
            def _():
                remote(esend.at[q], erecv.at[d], es.at[q, tt], er.at[d], g, e, tt).start()

            @pl.when(here)
            def _():
                erecv[d] = esend[q]

    owu[...] = nn(xt[...], all_up).astype(BF16)
    stores.append(pltpu.make_async_copy(owu, gwu_hbm.at[0], o_sem.at[1]))
    stores[1].start()
    for k in range(1, n):
        p = lax.rem(d + k, n)
        remote(dsc.at[p], dsc.at[p], ss.at[p], sr.at[p], p, e, t).wait_recv()
    owd[...] = nn(dsc[...].reshape(n * rows, hid).T, ys[...]).astype(BF16)
    stores.append(pltpu.make_async_copy(owd, gwd_hbm.at[0], o_sem.at[2]))
    stores[2].start()

    gate_sum = gsend[0:1, 0:cap]
    for k in range(1, tn):
        p = lax.rem(t + k, tn)
        remote(gsend, grecv.at[p], gs.at[p], gr.at[p], d, e, p).wait_recv()
        gate_sum = gate_sum + grecv[p, 0:1, 0:cap]
    gg_ref[...] = gate_sum

    for s in range(n):
        @pl.when(jnp.logical_not(jnp.logical_and(s == d, mine)))
        def _():
            remote(esend.at[0], erecv.at[s], es.at[0, 0], er.at[s], d, e, t).wait_recv()
        wide = erecv[s].astype(F32)
        gt_ref[:, s * bw:s * bw + bw // 2] = wide[:tl].astype(BF16)
        gt_ref[:, s * bw + bw // 2:(s + 1) * bw] = wide[tl:].astype(BF16)

    for c in to_owner + to_all:
        c.wait_send()
    for q in range(half):
        for tt in range(tn):
            @pl.when(jnp.logical_not(jnp.logical_and(t * half + q == d, t == tt)))
            def _():
                remote(esend.at[q], erecv.at[d], es.at[q, tt], er.at[d], d, e, tt).wait_send()
    for c in stores:
        c.wait()


def shards(n, ex, tn, tokens, grad_out, slot_token, slot_count, slot_gate, w_gate, w_up, w_down):
    tl, width = tokens.shape
    bw, hid = w_gate.shape[1:]
    rows = ex * tl
    all_rows = n * rows
    half = n // tn
    chunks = min(n, 4)
    vmem = pl.BlockSpec(memory_space=pltpu.VMEM)
    anywhere = pl.BlockSpec(memory_space=pl.ANY)
    dma = pltpu.SemaphoreType.DMA
    return pl.pallas_call(
        functools.partial(kernel, n, ex, tn),
        out_shape=(
            jax.ShapeDtypeStruct((tl, width), BF16),
            jax.ShapeDtypeStruct(slot_gate.shape, F32),
            jax.ShapeDtypeStruct(w_gate.shape, BF16),
            jax.ShapeDtypeStruct(w_up.shape, BF16),
            jax.ShapeDtypeStruct(w_down.shape, BF16),
        ),
        in_specs=[vmem, vmem, vmem, pl.BlockSpec(memory_space=pltpu.SMEM), vmem]
        + [anywhere] * 3,
        out_specs=(vmem, vmem, anywhere, anywhere, anywhere),
        scratch_shapes=[
            pltpu.VMEM((bw, hid), BF16),
            pltpu.VMEM((bw, hid), BF16),
            pltpu.VMEM((hid, bw), BF16),
            pltpu.VMEM((bw, hid), BF16),
            pltpu.VMEM((bw, hid), BF16),
            pltpu.VMEM((hid, bw), BF16),
            pltpu.VMEM((n, 2 * tl, bw), BF16),
            pltpu.VMEM((n, ex, 2 * tl, bw), BF16),
            pltpu.VMEM((all_rows, bw), BF16),
            pltpu.VMEM((all_rows, bw), BF16),
            pltpu.VMEM((bw, all_rows), BF16),
            pltpu.VMEM((3, n, rows, hid), BF16),
            pltpu.VMEM((3, n, rows, hid), BF16),
            pltpu.VMEM((n, 2, rows, hid), BF16),
            pltpu.VMEM((n, rows, hid), BF16),
            pltpu.VMEM((ex * tn, half * tl, bw), BF16),
            pltpu.VMEM((ex * tn, half * tl, bw), BF16),
            pltpu.VMEM((half, 2 * tl, bw // 2), BF16),
            pltpu.VMEM((n, 2 * tl, bw // 2), BF16),
            pltpu.VMEM((8, 128), F32),
            pltpu.VMEM((tn, 8, 128), F32),
            dma((3,)), dma((3,)),
            dma((n,)), dma((n,)),
            dma((chunks, ex)), dma((chunks, ex)),
            dma((3, n)), dma((3, n)),
            dma((n,)), dma((n,)),
            dma((n,)), dma((n,)),
            dma((ex * tn,)), dma((ex * tn,)),
            dma((half, tn)), dma((n,)),
            dma((tn,)), dma((tn,)),
        ],
        compiler_params=pltpu.CompilerParams(
            collective_id=0, has_side_effects=True, vmem_limit_bytes=48 * 1024 * 1024
        ),
    )(tokens, grad_out, slot_token, slot_count, slot_gate, w_gate, w_up, w_down)


def solution(mesh):
    n, ex, tn = (mesh.shape[a] for a in ("dp", "expert", "tensor"))
    return jax.shard_map(
        functools.partial(shards, n, ex, tn),
        mesh=mesh,
        in_specs=(
            P(("dp", "expert"), None),
            P(("dp", "expert"), None),
            P(("dp", "expert"), None),
            P(("dp", "expert")),
            P(("dp", "expert"), None),
            P("expert", "dp", "tensor"),
            P("expert", "dp", "tensor"),
            P("expert", "tensor", "dp"),
        ),
        out_specs=(
            P(("dp", "expert"), None),
            P(("dp", "expert"), None),
            P("expert", "dp", "tensor"),
            P("expert", "dp", "tensor"),
            P("expert", "tensor", "dp"),
        ),
        check_vma=False,
    )
```

time: 282 us -> 50.8 us (0.18)
  waiting for transfers between devices: 172 us -> 0 us
  blocking collectives: 60.7 us -> 0 us
  Pallas kernels: 0 us -> 40.3 us
  matrix products: 16.8 us -> 0 us
  between operations: 14.6 us -> 1.35 us
  starting transfers between devices: 8.49 us -> 0 us
  local copies, waits for them, and re-layouts: 5.2 us -> 8.86 us
  other arithmetic: 3.54 us -> 0 us
    all_gather x3 -> x0, waiting for transfers between devices: 170 us -> none  [the longest x1 61.3 us: shards(): lax.all_gather(w_gate, 'dp', axis=1, tiled=True)]
    all_gather x5 -> x0, blocking collectives: 55.8 us -> none  [the longest x1 16.1 us: shards(): lax.all_gather(d_gate, 'dp', axis=0, tiled=True)]
    pallas_call x0 -> x1, Pallas kernels: none -> 40.3 us  [shards(): pl.pallas_call(functools.partial(kernel, n, ex, tn), out_shape=(jax.Shape...]
    dot_general x8 -> x0, matrix products: 16.8 us -> none  [the longest x1 3.22 us: shards(): jnp.einsum('cnd,ndf->ncf', blocks_x, full_gate[0].reshape(dp_count, block...]
    all_to_all x2 -> x0, starting transfers between devices: 8.33 us -> none  [the longest x1 4.91 us: shards(): lax.all_to_all(rows_x, 'dp', split_axis=1, concat_axis=0, tiled=True)]
    unnamed x19, local copies, waits for them, and re-layouts: 2.34 us -> 8.86 us
    psum x1 -> x0, blocking collectives: 4.92 us -> none  [shards(): gate_total = lax.psum(gate_part_sum, 'tensor')]
  transfers between devices with their start and end apart: 7 -> 0, of which waited for: 4 -> 0; matrix products, arithmetic and copies ran while one was open for 8% -> 0% of each run, Pallas kernels for 0% -> 0%
where the time goes in v1:
time: 50.8 us; the launch traced here: 50.5 us
  Pallas kernels  40.3 us (79%)
  local copies, waits for them, and re-layouts  8.86 us (17%)
  between operations  1.35 us (3%)
    pallas_call x1, Pallas kernels, shards(): pl.pallas_call(functools.partial(kernel, n, ex, tn), out_shape=(jax.Shape...  40.3 us
    unnamed x19, local copies, waits for them, and re-layouts  8.86 us

profile of v1, /device:TPU:0, one launch (start us, length us, event | category | flops | bytes accessed | tf_op | source)
XLA Modules:
  0.0 50.5 jit_solution(16677264796940680504)
XLA Ops:
  0.6 0.0 copy-start.6
  0.6 0.0 copy-start.5
  1.3 0.0 copy-done.6
  1.3 0.0 copy-done.5
  1.3 0.0 copy-start
  1.3 1.1 %copy-done = bf16[1,1024,384]{2,1,0:T(8,128)(2,1)S(1)} copy-done((bf16[1,1024,384]{2,1,0:T(8,128)(2,1)S(1)}, bf16[1,1024,384]{2,1,0:T(8,128)(2,1)}, u32[]{:S(2)}) %copy-start) | copy-done | bytes 786456
  2.5 0.0 copy-start.1
  2.5 1.1 %copy-done.1 = bf16[1,1024,384]{2,1,0:T(8,128)(2,1)S(1)} copy-done((bf16[1,1024,384]{2,1,0:T(8,128)(2,1)S(1)}, bf16[1,1024,384]{2,1,0:T(8,128)(2,1)}, u32[]{:S(2)}) %copy-start.1) | copy-done | bytes 786456
  3.6 0.0 copy-start.2
  3.6 1.1 %copy-done.2 = bf16[1,384,1024]{2,1,0:T(8,128)(2,1)S(1)} copy-done((bf16[1,384,1024]{2,1,0:T(8,128)(2,1)S(1)}, bf16[1,384,1024]{2,1,0:T(8,128)(2,1)}, u32[]{:S(2)}) %copy-start.2) | copy-done | bytes 786456
  4.7 0.0 copy-start.3
  4.7 0.8 %copy-done.3 = bf16[8,4096]{1,0:T(8,128)(2,1)S(1)} copy-done((bf16[8,4096]{1,0:T(8,128)(2,1)S(1)}, bf16[8,4096]{1,0:T(8,128)(2,1)}, u32[]{:S(2)}) %copy-start.3) | copy-done | bytes 65560
  5.6 0.0 copy-start.4
  5.6 0.8 %copy-done.4 = bf16[8,4096]{1,0:T(8,128)(2,1)S(1)} copy-done((bf16[8,4096]{1,0:T(8,128)(2,1)S(1)}, bf16[8,4096]{1,0:T(8,128)(2,1)}, u32[]{:S(2)}) %copy-start.4) | copy-done | bytes 65560
  6.4 40.3 %shard_map.119 = (bf16[8,4096]{1,0:T(8,128)(2,1)S(1)}, f32[1,32]{1,0:T(1,128)S(1)}, bf16[1,1024,384]{2,1,0:T(8,128)(2,1)S(1)}, bf16[1,1024,384]{2,1,0:T(8,128)(2,1)S(1)}, bf16[1,384,1024]{2,1,0:T(8,128)(2,1)S(1)}) custom-call(bf16[8,4096]{1,0:T(8,128)(2,1)S(1)} %copy-done.3, bf16[8,4096]{1,0:T(8,128)(2,1)S(1)} %copy-done.4, s32[1,32]{1,0:T(1,128)S(1)} %copy-done.5, ...), custom_call_target="tpu_custom_call" | custom-call | tf_op jit(solution)/shard_map/pallas_call | solution.py:265
  46.7 0.6 %copy.19 = bf16[8,4096]{1,0:T(8,128)(2,1)} copy(bf16[8,4096]{1,0:T(8,128)(2,1)S(1)} %get-tuple-element.10) | data formatting | bytes 131072
  47.4 0.5 %copy.20 = f32[1,32]{1,0:T(1,128)} copy(f32[1,32]{1,0:T(1,128)S(1)} %get-tuple-element.11) | data formatting | bytes 256
  47.9 0.9 %copy.21 = bf16[1,1024,384]{2,1,0:T(8,128)(2,1)} copy(bf16[1,1024,384]{2,1,0:T(8,128)(2,1)S(1)} %get-tuple-element.12) | data formatting | bytes 1572864
  48.7 0.9 %copy.22 = bf16[1,1024,384]{2,1,0:T(8,128)(2,1)} copy(bf16[1,1024,384]{2,1,0:T(8,128)(2,1)S(1)} %get-tuple-element.13) | data formatting | bytes 1572864
  49.6 0.9 %copy.23 = bf16[1,384,1024]{2,1,0:T(8,128)(2,1)} copy(bf16[1,384,1024]{2,1,0:T(8,128)(2,1)S(1)} %get-tuple-element.14) | data formatting | bytes 1572864
Async XLA Ops:
  0.6 0.7 %copy-start.6 = (f32[1,32]{1,0:T(1,128)S(1)}, f32[1,32]{1,0:T(1,128)}, u32[]{:S(2)}) copy-start(f32[1,32]{1,0:T(1,128)} %gate_ref.1) | copy-start | bytes 388
  0.6 0.7 %copy-start.5 = (s32[1,32]{1,0:T(1,128)S(1)}, s32[1,32]{1,0:T(1,128)}, u32[]{:S(2)}) copy-start(s32[1,32]{1,0:T(1,128)} %slot_ref.1) | copy-start | bytes 388
  1.3 1.1 %copy-start = (bf16[1,1024,384]{2,1,0:T(8,128)(2,1)S(1)}, bf16[1,1024,384]{2,1,0:T(8,128)(2,1)}, u32[]{:S(2)}) copy-start(bf16[1,1024,384]{2,1,0:T(8,128)(2,1)} %wg_hbm.1) | copy-start | bytes 2359300
  2.5 1.1 %copy-start.1 = (bf16[1,1024,384]{2,1,0:T(8,128)(2,1)S(1)}, bf16[1,1024,384]{2,1,0:T(8,128)(2,1)}, u32[]{:S(2)}) copy-start(bf16[1,1024,384]{2,1,0:T(8,128)(2,1)} %wu_hbm.1) | copy-start | bytes 2359300
  3.6 1.1 %copy-start.2 = (bf16[1,384,1024]{2,1,0:T(8,128)(2,1)S(1)}, bf16[1,384,1024]{2,1,0:T(8,128)(2,1)}, u32[]{:S(2)}) copy-start(bf16[1,384,1024]{2,1,0:T(8,128)(2,1)} %wd_hbm.1) | copy-start | bytes 2359300
  4.7 0.8 %copy-start.3 = (bf16[8,4096]{1,0:T(8,128)(2,1)S(1)}, bf16[8,4096]{1,0:T(8,128)(2,1)}, u32[]{:S(2)}) copy-start(bf16[8,4096]{1,0:T(8,128)(2,1)} %x_ref.1) | copy-start | bytes 196612
  5.6 0.8 %copy-start.4 = (bf16[8,4096]{1,0:T(8,128)(2,1)S(1)}, bf16[8,4096]{1,0:T(8,128)(2,1)}, u32[]{:S(2)}) copy-start(bf16[8,4096]{1,0:T(8,128)(2,1)} %dy_ref.1) | copy-start | bytes 196612

commit v2 on v1

--- a/solution.py
+++ b/solution.py
@@ -22,11 +22,11 @@
 
 def kernel(
     n, ex, tn,
-    x_ref, dy_ref, slot_ref, count_ref, gate_ref, wg_hbm, wu_hbm, wd_hbm,
-    gt_ref, gg_ref, gwg_hbm, gwu_hbm, gwd_hbm,
-    wg, wu, wd, owg, owu, owd, src, full, xs, ys, xt, ps, pr, dgu, dsc,
+    x_hbm, dy_hbm, slot_ref, count_ref, gate_ref, wg_hbm, wu_hbm, wd_hbm,
+    gt_ref, gg_ref, xt, ys, ag_ref, au_ref, st_ref,
+    x_ref, dy_ref, wg, wu, wd, src, full, xs, ps, pr, dgu, dsc,
     dsend, drecv, esend, erecv, gsend, grecv,
-    w_sem, o_sem, a1s, a1r, a2s, a2r, bs, br, cs, cr, ss, sr, ds_, dr, es, er, gs, gr,
+    t_sem, w_sem, a1s, a1r, a2s, a2r, bs, br, cs, cr, ss, sr, ds_, dr, es, er, gs, gr,
 ):
     d = lax.axis_index("dp")
     e = lax.axis_index("expert")
@@ -46,6 +46,12 @@
             device_id=(dd, ee, tt), device_id_type=MESH,
         )
 
+    rows_in = [
+        pltpu.make_async_copy(x_hbm, x_ref, t_sem.at[0]),
+        pltpu.make_async_copy(dy_hbm, dy_ref, t_sem.at[1]),
+    ]
+    for load in rows_in:
+        load.start()
     barrier = pltpu.get_barrier_semaphore()
     greeted = 0
     for dd in range(n):
@@ -68,6 +74,8 @@
     for load in loads:
         load.start()
 
+    for load in rows_in:
+        load.wait()
     for b in range(n):
         cols = slice(b * bw, (b + 1) * bw)
         both = jnp.concatenate([x_ref[:, cols].astype(F32), dy_ref[:, cols].astype(F32)], axis=0)
@@ -84,47 +92,59 @@
         c.start()
         to_dp.append(c)
     to_expert = []
-    for k in range(chunks):
-        chunk = lax.rem(d // per + k, chunks)
-        for q in range(per):
-            g = chunk * per + q
-            if per == 1:
-                if k:
-                    remote(src.at[g], full.at[g, e], a1s.at[g], a1r.at[g], g, e, t).wait_recv()
-            else:
-                @pl.when(g != d)
-                def _():
-                    remote(src.at[g], full.at[g, e], a1s.at[g], a1r.at[g], g, e, t).wait_recv()
-        span = pl.ds(chunk * per, per)
-        for j in range(1, ex):
-            p = lax.rem(e + j, ex)
-            c = remote(full.at[span, e], full.at[span, e], a2s.at[chunk, p], a2r.at[chunk, e], d, p, t)
-            c.start()
-            to_expert.append(c)
-    for k in range(chunks):
-        chunk = lax.rem(d // per + k, chunks)
-        span = pl.ds(chunk * per, per)
-        for j in range(1, ex):
-            p = lax.rem(e + j, ex)
-            remote(full.at[span, p], full.at[span, p], a2s.at[chunk, p], a2r.at[chunk, p], d, p, t).wait_recv()
+    to_owner = []
+    work = ((xs, wg, nn), (xs, wu, nn), (ys, wd, nt))
+
+    def send_product(i, g):
+        return remote(ps.at[i, g], pr.at[i, d], bs.at[i, g], br.at[i, d], g, e, t)
+
+    for step in range(chunks + 1):
+        if step < chunks:
+            chunk = lax.rem(d // per + step, chunks)
+            for q in range(per):
+                g = chunk * per + q
+                if per == 1:
+                    if step:
+                        remote(src.at[g], full.at[g, e], a1s.at[g], a1r.at[g], g, e, t).wait_recv()
+                else:
+                    @pl.when(g != d)
+                    def _():
+                        remote(src.at[g], full.at[g, e], a1s.at[g], a1r.at[g], g, e, t).wait_recv()
+            span = pl.ds(chunk * per, per)
+            for j in range(1, ex):
+                p = lax.rem(e + j, ex)
+                c = remote(full.at[span, e], full.at[span, e], a2s.at[chunk, p], a2r.at[chunk, e], d, p, t)
+                c.start()
+                to_expert.append(c)
+        if step:
+            chunk = lax.rem(d // per + step - 1, chunks)
+            span = pl.ds(chunk * per, per)
+            for j in range(1, ex):
+                p = lax.rem(e + j, ex)
+                remote(full.at[span, p], full.at[span, p], a2s.at[chunk, p], a2r.at[chunk, p], d, p, t).wait_recv()
+            place = pl.ds(pl.multiple_of(chunk * (per * rows), per * rows), per * rows)
+            wide = full[span].astype(F32)
+            xs[place, :] = wide[:, :, :tl].reshape(per * rows, bw).astype(BF16)
+            ys[place, :] = wide[:, :, tl:].reshape(per * rows, bw).astype(BF16)
+            for i, (act, w, mul) in enumerate(work):
+                if step == 1:
+                    loads[i].wait()
+                ps[i, span] = mul(act[place, :], w[...]).astype(BF16).reshape(per, rows, hid)
+                for q in range(per):
+                    g = chunk * per + q
+                    if per == 1:
+                        if step > 1:
+                            c = send_product(i, g)
+                            c.start()
+                            to_owner.append(c)
+                    else:
+                        @pl.when(g != d)
+                        def _():
+                            send_product(i, g).start()
     for c in to_dp:
         c.wait_send()
     for c in to_expert:
         c.wait_send()
-    for g in range(n):
-        wide = full[g].astype(F32)
-        xs[g * rows:(g + 1) * rows, :] = wide[:, :tl].reshape(rows, bw).astype(BF16)
-        ys[g * rows:(g + 1) * rows, :] = wide[:, tl:].reshape(rows, bw).astype(BF16)
-
-    to_owner = []
-    for i, (act, w, mul) in enumerate(((xs, wg, nn), (xs, wu, nn), (ys, wd, nt))):
-        loads[i].wait()
-        ps[i] = mul(act[...], w[...]).astype(BF16).reshape(n, rows, hid)
-        for k in range(1, n):
-            p = lax.rem(d + k, n)
-            c = remote(ps.at[i, p], pr.at[i, d], bs.at[i, p], br.at[i, d], p, e, t)
-            c.start()
-            to_owner.append(c)
     xt[...] = xs[...].T
 
     iota_slot = lax.broadcasted_iota(jnp.int32, (1, cap), 1)
@@ -155,11 +175,6 @@
         c.start()
         to_all.append(c)
     dsc[d] = (gate_tok * hidden).astype(BF16)
-    for k in range(1, n):
-        p = lax.rem(d + k, n)
-        c = remote(dsc.at[d], dsc.at[d], ss.at[p], sr.at[d], p, e, t)
-        c.start()
-        to_all.append(c)
     terms = jnp.sum(hidden * back, axis=1, keepdims=True)
     gsend[0:1, 0:cap] = jnp.where(
         live, jnp.sum(jnp.where(holds, terms, 0.0), axis=0, keepdims=True), 0.0
@@ -173,6 +188,11 @@
     for k in range(1, n):
         p = lax.rem(d + k, n)
         remote(dgu.at[p], dgu.at[p], cs.at[p], cr.at[p], p, e, t).wait_recv()
+    for k in range(1, n):
+        p = lax.rem(d + k, n)
+        c = remote(dsc.at[d], dsc.at[d], ss.at[p], sr.at[d], p, e, t)
+        c.start()
+        to_all.append(c)
     all_gate = dgu[:, 0].reshape(n * rows, hid)
     all_up = dgu[:, 1].reshape(n * rows, hid)
     d_rows = (nt(all_gate, wg[...]) + nt(all_up, wu[...])).reshape(n, ex, tl, bw)
@@ -189,9 +209,8 @@
                 c.start()
                 to_all.append(c)
 
-    owg[...] = nn(xt[...], all_gate).astype(BF16)
-    stores = [pltpu.make_async_copy(owg, gwg_hbm.at[0], o_sem.at[0])]
-    stores[0].start()
+    ag_ref[...] = all_gate
+    au_ref[...] = all_up
 
     total = dsend[me].astype(F32)
     for ee in range(ex):
@@ -216,15 +235,10 @@
             def _():
                 erecv[d] = esend[q]
 
-    owu[...] = nn(xt[...], all_up).astype(BF16)
-    stores.append(pltpu.make_async_copy(owu, gwu_hbm.at[0], o_sem.at[1]))
-    stores[1].start()
     for k in range(1, n):
         p = lax.rem(d + k, n)
         remote(dsc.at[p], dsc.at[p], ss.at[p], sr.at[p], p, e, t).wait_recv()
-    owd[...] = nn(dsc[...].reshape(n * rows, hid).T, ys[...]).astype(BF16)
-    stores.append(pltpu.make_async_copy(owd, gwd_hbm.at[0], o_sem.at[2]))
-    stores[2].start()
+    st_ref[...] = dsc[...].reshape(n * rows, hid).T
 
     gate_sum = gsend[0:1, 0:cap]
     for k in range(1, tn):
@@ -241,6 +255,10 @@
         gt_ref[:, s * bw:s * bw + bw // 2] = wide[:tl].astype(BF16)
         gt_ref[:, s * bw + bw // 2:(s + 1) * bw] = wide[tl:].astype(BF16)
 
+    if per > 1:
+        for i in range(3):
+            for k in range(1, n):
+                send_product(i, lax.rem(d + k, n)).wait_send()
     for c in to_owner + to_all:
         c.wait_send()
     for q in range(half):
@@ -248,7 +266,30 @@
             @pl.when(jnp.logical_not(jnp.logical_and(t * half + q == d, t == tt)))
             def _():
                 remote(esend.at[q], erecv.at[d], es.at[q, tt], er.at[d], d, e, tt).wait_send()
-    for c in stores:
+
+
+def weight_grads(
+    gt_in, gg_in, xt, ys, ag, au, st, gt_hbm, gg_hbm, gwg_hbm, gwu_hbm, gwd_hbm, owg, owu, owd, sem
+):
+    copies = [
+        pltpu.make_async_copy(gt_in, gt_hbm, sem.at[0]),
+        pltpu.make_async_copy(gg_in, gg_hbm, sem.at[1]),
+    ]
+    for c in copies:
+        c.start()
+    work = ((xt, ag, owg, gwg_hbm), (xt, au, owu, gwu_hbm), (st, ys, owd, gwd_hbm))
+    for i, (left, right, held, out) in enumerate(work):
+        tall = left.shape[0]
+        piece = tall // 2
+        for j in range(2):
+            span = slice(j * piece, (j + 1) * piece)
+            held[span, :] = nn(left[span, :], right[...]).astype(BF16)
+            c = pltpu.make_async_copy(
+                held.at[span], out.at[0, span], sem.at[2 + 2 * i + j]
+            )
+            c.start()
+            copies.append(c)
+    for c in copies:
         c.wait()
 
 
@@ -260,32 +301,36 @@
     half = n // tn
     chunks = min(n, 4)
     vmem = pl.BlockSpec(memory_space=pltpu.VMEM)
-    anywhere = pl.BlockSpec(memory_space=pl.ANY)
+    hbm = pl.BlockSpec(memory_space=pltpu.HBM)
+    outs = (
+        jax.ShapeDtypeStruct((tl, width), BF16),
+        jax.ShapeDtypeStruct(slot_gate.shape, F32),
+        jax.ShapeDtypeStruct(w_gate.shape, BF16),
+        jax.ShapeDtypeStruct(w_up.shape, BF16),
+        jax.ShapeDtypeStruct(w_down.shape, BF16),
+    )
     dma = pltpu.SemaphoreType.DMA
-    return pl.pallas_call(
+    results = pl.pallas_call(
         functools.partial(kernel, n, ex, tn),
-        out_shape=(
-            jax.ShapeDtypeStruct((tl, width), BF16),
-            jax.ShapeDtypeStruct(slot_gate.shape, F32),
-            jax.ShapeDtypeStruct(w_gate.shape, BF16),
-            jax.ShapeDtypeStruct(w_up.shape, BF16),
-            jax.ShapeDtypeStruct(w_down.shape, BF16),
+        out_shape=outs[:2] + (
+            jax.ShapeDtypeStruct((bw, all_rows), BF16),
+            jax.ShapeDtypeStruct((all_rows, bw), BF16),
+            jax.ShapeDtypeStruct((all_rows, hid), BF16),
+            jax.ShapeDtypeStruct((all_rows, hid), BF16),
+            jax.ShapeDtypeStruct((hid, all_rows), BF16),
         ),
-        in_specs=[vmem, vmem, vmem, pl.BlockSpec(memory_space=pltpu.SMEM), vmem]
-        + [anywhere] * 3,
-        out_specs=(vmem, vmem, anywhere, anywhere, anywhere),
+        in_specs=[hbm, hbm, vmem, pl.BlockSpec(memory_space=pltpu.SMEM), vmem]
+        + [hbm] * 3,
+        out_specs=(vmem,) * 7,
         scratch_shapes=[
-            pltpu.VMEM((bw, hid), BF16),
-            pltpu.VMEM((bw, hid), BF16),
-            pltpu.VMEM((hid, bw), BF16),
+            pltpu.VMEM((tl, width), BF16),
+            pltpu.VMEM((tl, width), BF16),
             pltpu.VMEM((bw, hid), BF16),
             pltpu.VMEM((bw, hid), BF16),
             pltpu.VMEM((hid, bw), BF16),
             pltpu.VMEM((n, 2 * tl, bw), BF16),
             pltpu.VMEM((n, ex, 2 * tl, bw), BF16),
             pltpu.VMEM((all_rows, bw), BF16),
-            pltpu.VMEM((all_rows, bw), BF16),
-            pltpu.VMEM((bw, all_rows), BF16),
             pltpu.VMEM((3, n, rows, hid), BF16),
             pltpu.VMEM((3, n, rows, hid), BF16),
             pltpu.VMEM((n, 2, rows, hid), BF16),
@@ -296,7 +341,7 @@
             pltpu.VMEM((n, 2 * tl, bw // 2), BF16),
             pltpu.VMEM((8, 128), F32),
             pltpu.VMEM((tn, 8, 128), F32),
-            dma((3,)), dma((3,)),
+            dma((2,)), dma((3,)),
             dma((n,)), dma((n,)),
             dma((chunks, ex)), dma((chunks, ex)),
             dma((3, n)), dma((3, n)),
@@ -307,9 +352,22 @@
             dma((tn,)), dma((tn,)),
         ],
         compiler_params=pltpu.CompilerParams(
-            collective_id=0, has_side_effects=True, vmem_limit_bytes=48 * 1024 * 1024
+            collective_id=0, has_side_effects=True, vmem_limit_bytes=64 * 1024 * 1024 - 65536
         ),
     )(tokens, grad_out, slot_token, slot_count, slot_gate, w_gate, w_up, w_down)
+    return pl.pallas_call(
+        weight_grads,
+        out_shape=outs,
+        in_specs=[vmem] * 7,
+        out_specs=(hbm,) * 5,
+        scratch_shapes=[
+            pltpu.VMEM((bw, hid), BF16),
+            pltpu.VMEM((bw, hid), BF16),
+            pltpu.VMEM((hid, bw), BF16),
+            dma((8,)),
+        ],
+        compiler_params=pltpu.CompilerParams(vmem_limit_bytes=64 * 1024 * 1024 - 65536),
+    )(*results)
 
 
 def solution(mesh):

time: 50.8 us -> 44.8 us (0.88)
  local copies, waits for them, and re-layouts: 8.86 us -> 0 us
  Pallas kernels: 40.3 us -> 43.3 us
    unnamed x19 -> x0, local copies, waits for them, and re-layouts: 8.86 us -> none
    pallas_call x1 -> x2, Pallas kernels: 40.3 us -> 43.3 us  [the longest x1 40.4 us: shards(): pl.pallas_call(functools.partial(kernel, n, ex, tn), out_shape=outs[:2] +...]
where the time goes in v2:
time: 44.8 us; the launch traced here: 44.6 us
  Pallas kernels  43.3 us (97%)
  between operations  1.29 us (3%)
    pallas_call x1, Pallas kernels, shards(): pl.pallas_call(functools.partial(kernel, n, ex, tn), out_shape=outs[:2] +...  40.4 us
    pallas_call x1, Pallas kernels, shards(): pl.pallas_call(weight_grads, out_shape=outs, in_specs=[vmem] * 7, out_spe...  2.91 us

profile of v2, /device:TPU:0, one launch (start us, length us, event | category | flops | bytes accessed | tf_op | source)
XLA Modules:
  0.0 44.6 jit_solution(10955820475523911262)
XLA Ops:
  1.3 40.4 %shard_map.119 = (bf16[8,4096]{1,0:T(8,128)(2,1)}, f32[1,32]{1,0:T(1,128)}, bf16[1024,128]{1,0:T(8,128)(2,1)}, bf16[128,1024]{1,0:T(8,128)(2,1)}, bf16[128,384]{...) custom-call(bf16[8,4096]{1,0:T(8,128)(2,1)} %x_hbm.1, bf16[8,4096]{1,0:T(8,128)(2,1)} %dy_hbm.1, ...), custom_call_target="tpu_custom_call" | custom-call | tf_op jit(solution)/shard_map/pallas_call | solution.py:313
  41.7 2.9 %shard_map.120 = (bf16[8,4096]{1,0:T(8,128)(2,1)}, f32[1,32]{1,0:T(1,128)}, bf16[1,1024,384]{2,1,0:T(8,128)(2,1)}, bf16[1,1024,384]{2,1,0:T(8,128)(2,1)}, bf16[1,384,1024]{2,1,0:T(8,128)(2,1)}) custom-call(bf16[8,4096]{1,0:T(8,128)(2,1)} %get-tuple-element.12.gt_in, f32[1,32]{1,0:T(1,128)} %get-tuple-element.13.gg_in, ...), custom_call_target="tpu_custom_call" | custom-call | tf_op jit(solution)/shard_map/pallas_call | solution.py:358

commit v3 on v2

--- a/solution.py
+++ b/solution.py
@@ -86,7 +86,7 @@
     pl.semaphore_wait(barrier, greeted)
 
     to_dp = []
-    for k in range(1, n):
+    for k in reversed(range(1, n)):
         p = lax.rem(d + k, n)
         c = remote(src.at[p], full.at[d, e], a1s.at[p], a1r.at[d], p, e, t)
         c.start()

time: 44.8 us -> 43.4 us (0.969)
  Pallas kernels: 43.3 us -> 41.9 us
    pallas_call x1, Pallas kernels: 40.4 us -> 39 us  [shards(): pl.pallas_call(functools.partial(kernel, n, ex, tn), out_shape=outs[:2] +...]
where the time goes in v3:
time: 43.4 us; the launch traced here: 43.2 us
  Pallas kernels  41.9 us (97%)
  between operations  1.29 us (3%)
    pallas_call x1, Pallas kernels, shards(): pl.pallas_call(functools.partial(kernel, n, ex, tn), out_shape=outs[:2] +...  39 us
    pallas_call x1, Pallas kernels, shards(): pl.pallas_call(weight_grads, out_shape=outs, in_specs=[vmem] * 7, out_spe...  2.91 us

profile of v3, /device:TPU:0, one launch (start us, length us, event | category | flops | bytes accessed | tf_op | source)
XLA Modules:
  0.0 43.2 jit_solution(7229552912800218992)
XLA Ops:
  1.3 39.0 %shard_map.119 = (bf16[8,4096]{1,0:T(8,128)(2,1)}, f32[1,32]{1,0:T(1,128)}, bf16[1024,128]{1,0:T(8,128)(2,1)}, bf16[128,1024]{1,0:T(8,128)(2,1)}, bf16[128,384]{...) custom-call(bf16[8,4096]{1,0:T(8,128)(2,1)} %x_hbm.1, bf16[8,4096]{1,0:T(8,128)(2,1)} %dy_hbm.1, ...), custom_call_target="tpu_custom_call" | custom-call | tf_op jit(solution)/shard_map/pallas_call | solution.py:313
  40.3 2.9 %shard_map.120 = (bf16[8,4096]{1,0:T(8,128)(2,1)}, f32[1,32]{1,0:T(1,128)}, bf16[1,1024,384]{2,1,0:T(8,128)(2,1)}, bf16[1,1024,384]{2,1,0:T(8,128)(2,1)}, bf16[1,384,1024]{2,1,0:T(8,128)(2,1)}) custom-call(bf16[8,4096]{1,0:T(8,128)(2,1)} %get-tuple-element.12.gt_in, f32[1,32]{1,0:T(1,128)} %get-tuple-element.13.gg_in, ...), custom_call_target="tpu_custom_call" | custom-call | tf_op jit(solution)/shard_map/pallas_call | solution.py:358
